TPU v7x, 256 devices: a whole 4x4x8 slice. The times are simulated.
256 devices in a mesh: gx: 8 (over z), gy: 8 (over y_lo, x), band: 4 (over y_hi, core).
Axes of the slice: x: 4, y: 4 (y_hi: 2, y_lo: 2; y = y_hi * 2 + y_lo), z: 8, core: 2. Of those that a mesh axis runs over, the one named last changes fastest.
Arguments:
- orbitals: float32 [8, 96, 288, 128], P('band', 'gx', 'gy'), may hold values from -60 to 60
- potential: float32 [96, 288, 128], P('gx', 'gy'), may hold values from -3 to 0
Outputs:
- rotated: float32 [8, 96, 288, 128], P('band', 'gx', 'gy')
- density: float32 [96, 288, 128], P('gx', 'gy')
All inputs are finite; a program needn't handle non-finite values.
Results may differ from a plain program's by a relative error of at most 0.00013.
Values sent between devices are 32-bit elements; how exact they have to be, the bound alone decides.
A program may use at most 64 MiB of HBM per device.

v0:
```python
import functools

import jax
import jax.numpy as jnp
from jax import lax
from jax.experimental import pallas as pl
from jax.experimental.pallas import tpu as pltpu
from jax.sharding import PartitionSpec as P

COEFFS = (
    -5369.0 / 1800.0,
    12.0 / 7.0,
    -15.0 / 56.0,
    10.0 / 189.0,
    -1.0 / 112.0,
    2.0 / 1925.0,
    -1.0 / 16632.0,
)
CENTER = 6.25
HALFWIDTH = 4.75
UPPER = 11.0
NB = 8
MESH = pl.DeviceIdType.MESH

LX = 12
LY = 36
ROWS = 2 * LY
HX = 6
HY = 16
PIECES = ((0, 16), (56, 16), (16, 40))
NP = len(PIECES)


def swap_pairs(cells):
    tiles = cells.reshape(-1, 8, 128)
    even = (lax.broadcasted_iota(jnp.int32, tiles.shape, 1) & 1) == 0
    return jnp.where(even, pltpu.roll(tiles, 7, 1), pltpu.roll(tiles, 1, 1)).reshape(cells.shape)


def filter_kernel(
    orb_ref, pot_ref, bands_ref, sums_ref,
    f0, f1, f2, f3, weight, pot, acc, app, swf, swa, gathered, accs, rows_a, rows_b, msg,
    xs, xr, ys, yr, ps, pr, gs, gr, ss, sr, ls,
):
    gx, gy, band = lax.axis_index("gx"), lax.axis_index("gy"), lax.axis_index("band")
    y_lo, x = gy // 4, gy % 4
    y_hi, core = band // 2, band % 2

    load_orb = pltpu.make_async_copy(orb_ref, f0.at[pl.ds(HX, LX), pl.ds(HY, ROWS)], ls.at[0])
    load_pot = pltpu.make_async_copy(pot_ref, pot, ls.at[1])
    load_orb.start()
    load_pot.start()

    group_a = [
        (lax.rem(gx + i, 8), gy, 2 * y_hi + (core if j == 0 else 1 - core))
        for j in range(2) for i in range(8) if i or j
    ]
    group_b = [
        (gx, 4 * (y_lo if a == 0 else 1 - y_lo) + lax.rem(x + i, 4), 2 * (y_hi if b == 0 else 1 - y_hi) + core)
        for b in range(2) for a in range(2) for i in range(4) if a or b or i
    ]
    barrier = pltpu.get_barrier_semaphore()
    for device in group_a + group_b:
        pl.semaphore_signal(barrier, inc=1, device_id=device, device_id_type=MESH)

    x_up, x_down = (lax.rem(gx + 1, 8), gy, band), (lax.rem(gx + 7, 8), gy, band)
    y_up, y_down = (gx, lax.rem(gy + 1, 8), band), (gx, lax.rem(gy + 7, 8), band)
    sibling = (gx, gy, 2 * y_hi + 1 - core)
    partner = (gx, gy, 2 * (1 - y_hi) + core)
    far = 2 * (1 - y_hi) + core
    near = 2 * y_hi + 1 - core
    last = 3 - band

    fields = (f0, f1, f2, f3)

    def remote(src, dst, send, recv, device):
        return pltpu.make_async_remote_copy(
            src_ref=src, dst_ref=dst, send_sem=send, recv_sem=recv, device_id=device, device_id_type=MESH
        )

    def x_copy(step, piece, side):
        field, (first, count) = fields[step], PIECES[piece]
        rows = pl.ds(HY + first, count)
        src, dst, device = ((HX, HX + LX, x_down), (LX, 0, x_up))[side]
        return remote(
            field.at[pl.ds(src, HX), rows], field.at[pl.ds(dst, HX), rows],
            xs.at[step, piece, side], xr.at[step, piece, side], device,
        )

    def y_copy(step, side):
        field = fields[step]
        src, dst, device = ((HY, HY + ROWS, y_down), (ROWS, 0, y_up))[side]
        return remote(
            field.at[pl.ds(HX, LX), pl.ds(src, HY)], field.at[pl.ds(HX, LX), pl.ds(dst, HY)],
            ys.at[step, side], yr.at[step, side], device,
        )

    def band_copy(kind, piece):
        first, count = PIECES[piece]
        mine = f3.at[pl.ds(HX, LX), pl.ds(HY + first, count)]
        rows = pl.ds(first, count)
        if kind == 2:
            src, slot = gathered.at[far, :, rows], far
        else:
            src, slot = mine, band
        return remote(
            src, gathered.at[slot, :, rows], gs.at[kind, piece], gr.at[kind, piece], partner if kind == 0 else sibling
        )

    def send_piece(step, piece):
        sides = (0,) if step == 3 else (0, 1)
        for side in sides:
            x_copy(step, piece, side).start()
        if piece == 0:
            y_copy(step, 0).start()
        if piece == 1 and step < 3:
            y_copy(step, 1).start()
        if step == 3:
            band_copy(0, piece).start()
            band_copy(1, piece).start()

    load_pot.wait()
    load_orb.wait()

    @pl.loop(0, LX)
    def _(layer):
        values = (pot[layer] - (CENTER + 1.5 * COEFFS[0])) * (1.0 / HALFWIDTH)
        weight[layer, pl.ds(0, LY, stride=2), :] = values
        weight[layer, pl.ds(1, LY, stride=2), :] = values

    pl.semaphore_wait(barrier, 30)
    for piece in range(NP):
        send_piece(0, piece)

    for step in range(3):
        field, following = fields[step], fields[step + 1]
        scale = 1.0 if step == 0 else 2.0
        coeffs = [-0.5 * scale * c / HALFWIDTH for c in COEFFS]

        @pl.loop(0, LX)
        def _(layer):
            f = field[HX + layer, pl.ds(HY, ROWS), :]
            total = scale * weight[layer] * f
            if step:
                total = total - fields[step - 1][HX + layer, pl.ds(HY, ROWS), :]
            for k in range(1, 7):
                total = total + coeffs[k] * (pltpu.roll(f, k, 1) + pltpu.roll(f, 128 - k, 1))
            acc[layer] = total

        y_copy(step, 0).wait_recv()
        y_copy(step, 1).wait_recv()

        @pl.loop(0, LX)
        def _(layer):
            total = acc[layer]
            for k in range(1, 7):
                below = field[HX + layer, pl.ds(HY - 2 * k, ROWS), :]
                above = field[HX + layer, pl.ds(HY + 2 * k, ROWS), :]
                total = total + coeffs[k] * (below + above)
            acc[layer] = total

        for piece, (first, count) in enumerate(PIECES):
            x_copy(step, piece, 0).wait_recv()
            x_copy(step, piece, 1).wait_recv()
            rows = pl.ds(HY + first, count)

            @pl.loop(0, LX)
            def _(layer):
                total = acc[layer, pl.ds(first, count), :]
                for k in range(1, 7):
                    total = total + coeffs[k] * (field[HX + layer - k, rows, :] + field[HX + layer + k, rows, :])
                following[HX + layer, rows, :] = total

            send_piece(step + 1, piece)

    coeffs = [-c / HALFWIDTH for c in COEFFS]

    @pl.loop(0, LX)
    def _(layer):
        f = f3[HX + layer, pl.ds(HY, ROWS), :]
        total = weight[layer] * f
        for k in range(1, 7):
            total = total + coeffs[k] * pltpu.roll(f, 128 - k, 1)
        acc[layer] = total
        swf[layer] = swap_pairs(f)

    for piece in (0, 1):
        band_copy(0, piece).wait_recv()
        band_copy(2, piece).start()
    y_copy(3, 0).wait_recv()

    @pl.loop(0, LX)
    def _(layer):
        total = acc[layer]
        for k in range(1, 7):
            total = total + coeffs[k] * f3[HX + layer, pl.ds(HY + 2 * k, ROWS), :]
        acc[layer] = total

    for piece, (first, count) in enumerate(PIECES):
        x_copy(3, piece, 0).wait_recv()

        @pl.loop(0, LX)
        def _(layer):
            total = acc[layer, pl.ds(first, count), :]
            for k in range(1, 7):
                total = total + coeffs[k] * f3[HX + layer + k, pl.ds(HY + first, count), :]
            app[layer, pl.ds(first, count), :] = total
            swa[layer, pl.ds(first, count), :] = swap_pairs(total)

    accs[...] = jnp.zeros_like(accs)

    def products(relative, slot, piece):
        first, count = PIECES[piece]
        rows = pl.ds(first, count)

        def body(layer, carry):
            if slot is None:
                g = f3[HX + layer, pl.ds(HY + first, count), :]
                gathered[band, layer, rows, :] = g
            else:
                g = gathered[slot, layer, rows, :]
            g = g.reshape(-1, 8, 128)
            mine = (f3[HX + layer, pl.ds(HY + first, count), :], swf[layer, rows, :], app[layer, rows, :], swa[layer, rows, :])
            return tuple(c + jnp.sum(m.reshape(-1, 8, 128) * g, axis=0) for c, m in zip(carry, mine))

        start = tuple(accs[pl.ds(8 * (4 * relative + i), 8), :] for i in range(4))
        for i, total in enumerate(lax.fori_loop(0, LX, body, start)):
            accs[pl.ds(8 * (4 * relative + i), 8), :] = total

    for piece in range(NP):
        products(0, None, piece)
    for piece in range(NP):
        band_copy(1, piece).wait_recv()
        products(1, near, piece)
    for piece in (0, 1):
        products(2, far, piece)
    for piece in (0, 1):
        band_copy(2, piece).wait_recv()
        products(3, last, piece)
    band_copy(0, 2).wait_recv()
    band_copy(2, 2).start()
    products(2, far, 2)
    band_copy(2, 2).wait_recv()
    products(3, last, 2)

    store = pltpu.make_async_copy(gathered, bands_ref, ls.at[2])
    store.start()

    highest = lax.Precision.HIGHEST
    by_row = lax.dot_general(
        jnp.ones((8, 128), jnp.float32), accs[...], (((1,), (1,)), ((), ())),
        precision=highest, preferred_element_type=jnp.float32,
    )
    source = lax.broadcasted_iota(jnp.int32, (128, 128), 0)
    target = lax.broadcasted_iota(jnp.int32, (128, 128), 1)
    place = (target == 32 * band + 2 * (source >> 3) + (source & 1)).astype(jnp.float32)
    msg[pl.ds(0, 8), :] = jnp.dot(by_row, place, precision=highest, preferred_element_type=jnp.float32)

    def sum_stage(stage, devices, me, rows):
        rows[pl.ds(me, 1), :] = msg[pl.ds(8 * stage, 1), :]
        copies = [
            remote(msg.at[pl.ds(8 * stage, 1)], rows.at[pl.ds(me, 1)], ss.at[stage, i], sr.at[stage, i], device)
            for i, device in enumerate(devices)
        ]
        for copy in copies:
            copy.start()
        for copy in copies:
            copy.wait_recv()
        return copies

    copies = sum_stage(0, group_a, 2 * gx + core, rows_a)
    total = jnp.sum(rows_a[...], axis=0, keepdims=True)
    msg[pl.ds(8, 8), :] = jnp.broadcast_to(total, (8, 128))
    copies = copies + sum_stage(1, group_b, 4 * (2 * y_hi + y_lo) + x, rows_b)
    total = jnp.sum(rows_b[...], axis=0, keepdims=True)
    sums_ref[...] = jnp.broadcast_to(total, (8, 128))

    for copy in copies:
        copy.wait_send()
    for step in range(4):
        for piece in range(NP):
            for side in (0, 1) if step < 3 else (0,):
                x_copy(step, piece, side).wait_send()
        for side in (0, 1) if step < 3 else (0,):
            y_copy(step, side).wait_send()
    for kind in range(3):
        for piece in range(NP):
            band_copy(kind, piece).wait_send()
    store.wait()


def rotate_kernel(bands_ref, sums_ref, rotated_ref, density_ref, splat, mix, squares):
    band = lax.axis_index("band")
    highest = lax.Precision.HIGHEST
    row = lax.broadcasted_iota(jnp.int32, (128, 128), 0)
    lane = lax.broadcasted_iota(jnp.int32, (128, 128), 1)
    diagonal = jnp.where(row == lane, jnp.broadcast_to(sums_ref[0:1, :], (128, 128)), 0.0)
    splat[...] = jnp.dot(
        diagonal, jnp.ones((128, 128), jnp.float32), precision=highest, preferred_element_type=jnp.float32
    ) * (1.0 / 3538944.0)

    def entry(kind, i, j):
        pair, other = i // 2, j // 2
        lane_of = 32 * pair + 2 * (4 * (pair ^ other) + 2 * kind + (i % 2 != j % 2)) + j % 2
        return jnp.broadcast_to(splat[lane_of : lane_of + 1, :], (8, 128))

    lower, inverse, pivot = {}, {}, {}
    for j in range(NB):
        d = entry(0, j, j)
        for k in range(j):
            d = d - lower[j, k] * lower[j, k]
        pivot[j] = 1.0 / jnp.sqrt(d)
        for i in range(j + 1, NB):
            v = entry(0, i, j)
            for k in range(j):
                v = v - lower[i, k] * lower[j, k]
            lower[i, j] = v * pivot[j]
    for j in range(NB):
        inverse[j, j] = pivot[j]
        for i in range(j + 1, NB):
            v = lower[i, j] * inverse[j, j]
            for k in range(j + 1, i):
                v = v + lower[i, k] * inverse[k, j]
            inverse[i, j] = -v * pivot[i]
    projected = {}
    for i in range(NB):
        for j in range(i + 1):
            projected[i, j] = projected[j, i] = entry(1, i, i) if i == j else 0.5 * (entry(1, i, j) + entry(1, j, i))
    factor = {}
    for i in range(NB):
        half = [sum((inverse[i, k] * projected[k, j] for k in range(1, i + 1)), inverse[i, 0] * projected[0, j]) for j in range(i + 1)]
        for j in range(i + 1):
            v = half[0] * inverse[j, 0]
            for k in range(1, j + 1):
                v = v + half[k] * inverse[j, k]
            v = v * (-HALFWIDTH / UPPER)
            factor[i, j] = factor[j, i] = v + (1.0 - CENTER / UPPER) if i == j else v
    even = (lax.broadcasted_iota(jnp.int32, (8, 128), 0) & 1) == 0
    for k in range(NB // 2):
        columns = {}
        for j in range(NB):
            for b in range(2):
                v = inverse[j, j] * factor[j, 2 * k + b]
                for i in range(j + 1, NB):
                    v = v + inverse[i, j] * factor[i, 2 * k + b]
                columns[j, b] = v
        for q in range(NB // 2):
            mix[8 * k + 2 * q] = jnp.where(even, columns[2 * q, 0], columns[2 * q + 1, 1])
            mix[8 * k + 2 * q + 1] = jnp.where(even, columns[2 * q + 1, 0], columns[2 * q, 1])

    @pl.loop(0, LX)
    def _(layer):
        for tile in range(ROWS // 8):
            rows = pl.ds(8 * tile, 8)
            parts = []
            for q in range(NB // 2):
                g = bands_ref[q, layer, rows, :]
                parts += [g, swap_pairs(g)]
            density = own = None
            for k in range(NB // 2):
                v = mix[8 * k] * parts[0]
                for n in range(1, 8):
                    v = v + mix[8 * k + n] * parts[n]
                density = v * v if density is None else density + v * v
                own = v if own is None else jnp.where(band == k, v, own)
            rotated_ref[layer, rows, :] = own
            squares[rows, :] = density
        density_ref[layer] = (
            squares[pl.ds(0, LY, stride=2), :] + squares[pl.ds(1, LY, stride=2), :]
        ) * (1.0 / NB)


def on_device(orbitals, potential):
    f32 = jnp.float32
    orb = orbitals.transpose(1, 2, 0, 3).reshape(LX, ROWS, 128)
    vmem = functools.partial(pltpu.VMEM, dtype=f32)
    field = vmem((LX + 2 * HX, ROWS + 2 * HY, 128))
    block = vmem((LX, ROWS, 128))
    dma = pltpu.SemaphoreType.DMA
    bands, sums = pl.pallas_call(
        filter_kernel,
        out_shape=(
            jax.ShapeDtypeStruct((4, LX, ROWS, 128), f32),
            jax.ShapeDtypeStruct((8, 128), f32),
        ),
        in_specs=[pl.BlockSpec(memory_space=pl.ANY)] * 2,
        out_specs=(pl.BlockSpec(memory_space=pl.ANY), pl.BlockSpec(memory_space=pltpu.VMEM)),
        scratch_shapes=[
            field, field, field, field, block, vmem((LX, LY, 128)), block, block, block, block,
            vmem((4, LX, ROWS, 128)), vmem((128, 128)), vmem((16, 128)), vmem((16, 128)), vmem((16, 128)),
            dma((4, NP, 2)), dma((4, NP, 2)), dma((4, 2)), dma((4, 2)), dma((1,)), dma((1,)),
            dma((3, NP)), dma((3, NP)), dma((2, 15)), dma((2, 15)), dma((3,)),
        ],
        compiler_params=pltpu.CompilerParams(
            collective_id=0, has_side_effects=True, vmem_limit_bytes=20 * 1024 * 1024
        ),
        name="filter_and_sums",
    )(orb, potential)
    rotated, density = pl.pallas_call(
        rotate_kernel,
        out_shape=(
            jax.ShapeDtypeStruct((LX, ROWS, 128), f32),
            jax.ShapeDtypeStruct((LX, LY, 128), f32),
        ),
        in_specs=[pl.BlockSpec(memory_space=pltpu.VMEM)] * 2,
        out_specs=(pl.BlockSpec(memory_space=pltpu.VMEM),) * 2,
        scratch_shapes=[vmem((128, 128)), vmem((32, 8, 128)), vmem((ROWS, 128))],
        compiler_params=pltpu.CompilerParams(vmem_limit_bytes=20 * 1024 * 1024),
        name="rotate_and_density",
    )(bands, sums)
    return rotated.reshape(LX, LY, 2, 128).transpose(2, 0, 1, 3), density


def solution(mesh):
    return jax.shard_map(
        on_device,
        mesh=mesh,
        in_specs=(P("band", "gx", "gy", None), P("gx", "gy", None)),
        out_specs=(P("band", "gx", "gy", None), P("gx", "gy", None)),
        check_vma=False,
    )
```

profile of v0, /device:TPU:1, one launch (start us, length us, event | category | flops | bytes accessed | tf_op | source)
XLA Modules:
  0.0 55.2 jit_solution(1905557588327860691)
XLA Ops:
  0.6 0.0 copy-start
  0.6 1.0 %copy-done = f32[2,12,36,128]{3,0,2,1:T(2,128)S(1)} copy-done((f32[2,12,36,128]{3,0,2,1:T(2,128)S(1)}, f32[2,12,36,128]{3,0,2,1:T(2,128)}, u32[]{:S(2)}) %copy-start) | copy-done | bytes 442392
  1.6 0.0 copy-start.1
  1.6 0.9 %copy-done.1 = f32[12,36,128]{2,1,0:T(8,128)S(1)} copy-done((f32[12,36,128]{2,1,0:T(8,128)S(1)}, f32[12,36,128]{2,1,0:T(8,128)}, u32[]{:S(2)}) %copy-start.1) | copy-done | bytes 221208
  2.6 49.8 %filter_and_sums.1 = (f32[4,12,72,128]{3,2,1,0:T(8,128)S(1)}, f32[8,128]{1,0:T(8,128)S(1)}) custom-call(f32[12,72,128]{2,1,0:T(8,128)S(1)} %bitcast.6, f32[12,36,128]{2,1,0:T(8,128)S(1)} %copy-done.1), custom_call_target="tpu_custom_call" | custom-call | tf_op jit(solution)/shard_map/filter_and_sums/pallas_call | solution.py:380
  52.4 2.7 %rotate_and_density.1 = (f32[12,72,128]{2,1,0:T(8,128)}, f32[12,36,128]{2,1,0:T(8,128)}) custom-call(f32[4,12,72,128]{3,2,1,0:T(8,128)S(1)} %get-tuple-element.6.bands_ref, f32[8,128]{1,0:T(8,128)S(1)} %get-tuple-element.7.sums_ref), custom_call_target="tpu_custom_call" | custom-call | tf_op jit(solution)/shard_map/rotate_and_density/pallas_call | solution.py:399
Async XLA Ops:
  0.6 1.0 %copy-start = (f32[2,12,36,128]{3,0,2,1:T(2,128)S(1)}, f32[2,12,36,128]{3,0,2,1:T(2,128)}, u32[]{:S(2)}) copy-start(f32[2,12,36,128]{3,0,2,1:T(2,128)} %param.2) | copy-start | bytes 1327108
  1.6 0.9 %copy-start.1 = (f32[12,36,128]{2,1,0:T(8,128)S(1)}, f32[12,36,128]{2,1,0:T(8,128)}, u32[]{:S(2)}) copy-start(f32[12,36,128]{2,1,0:T(8,128)} %pot_ref.1) | copy-start | bytes 663556
where the time goes:
time: 55.3 us; the launch traced here: 55.2 us
  Pallas kernels  52.6 us (95%)
  local copies, waits for them, and re-layouts  1.95 us (4%)
  between operations  0.65 us (1%)
    pallas_call x1, Pallas kernels, on_device(): pl.pallas_call(filter_kernel, out_shape=(jax.ShapeDtypeStruct((4, LX, ROW...  49.8 us
    pallas_call x1, Pallas kernels, on_device(): pl.pallas_call(rotate_kernel, out_shape=(jax.ShapeDtypeStruct((LX, ROWS,...  2.73 us
    unnamed x4, local copies, waits for them, and re-layouts  1.95 us

commit v1 on v0

--- a/solution.py
+++ b/solution.py
@@ -20,6 +20,7 @@
 HALFWIDTH = 4.75
 UPPER = 11.0
 NB = 8
+VMEM_BYTES = 60 * 1024 * 1024
 MESH = pl.DeviceIdType.MESH
 
 LX = 12
@@ -27,8 +28,10 @@
 ROWS = 2 * LY
 HX = 6
 HY = 16
-PIECES = ((0, 16), (56, 16), (16, 40))
+EDGE = 12
+PIECES = ((0, 16), (56, 16), (16, 24), (40, 16))
 NP = len(PIECES)
+PART = 3
 
 
 def swap_pairs(cells):
@@ -60,13 +63,12 @@
         for b in range(2) for a in range(2) for i in range(4) if a or b or i
     ]
     barrier = pltpu.get_barrier_semaphore()
-    for device in group_a + group_b:
-        pl.semaphore_signal(barrier, inc=1, device_id=device, device_id_type=MESH)
-
     x_up, x_down = (lax.rem(gx + 1, 8), gy, band), (lax.rem(gx + 7, 8), gy, band)
     y_up, y_down = (gx, lax.rem(gy + 1, 8), band), (gx, lax.rem(gy + 7, 8), band)
     sibling = (gx, gy, 2 * y_hi + 1 - core)
     partner = (gx, gy, 2 * (1 - y_hi) + core)
+    for device in (x_up, x_down, y_up, y_down, sibling, partner):
+        pl.semaphore_signal(barrier, inc=1, device_id=device, device_id_type=MESH)
     far = 2 * (1 - y_hi) + core
     near = 2 * y_hi + 1 - core
     last = 3 - band
@@ -89,9 +91,10 @@
 
     def y_copy(step, side):
         field = fields[step]
-        src, dst, device = ((HY, HY + ROWS, y_down), (ROWS, 0, y_up))[side]
+        src, dst, device = ((HY, HY + ROWS, y_down), (HY + ROWS - EDGE, HY - EDGE, y_up))[side]
+        layers = pl.ds(HX + LX // 2 * side, LX // 2) if step == 3 else pl.ds(HX, LX)
         return remote(
-            field.at[pl.ds(HX, LX), pl.ds(src, HY)], field.at[pl.ds(HX, LX), pl.ds(dst, HY)],
+            field.at[layers, pl.ds(src, EDGE)], field.at[layers, pl.ds(dst, EDGE)],
             ys.at[step, side], yr.at[step, side], device,
         )
 
@@ -113,7 +116,7 @@
             x_copy(step, piece, side).start()
         if piece == 0:
             y_copy(step, 0).start()
-        if piece == 1 and step < 3:
+        if piece == 1:
             y_copy(step, 1).start()
         if step == 3:
             band_copy(0, piece).start()
@@ -128,7 +131,7 @@
         weight[layer, pl.ds(0, LY, stride=2), :] = values
         weight[layer, pl.ds(1, LY, stride=2), :] = values
 
-    pl.semaphore_wait(barrier, 30)
+    pl.semaphore_wait(barrier, 6)
     for piece in range(NP):
         send_piece(0, piece)
 
@@ -184,17 +187,19 @@
         acc[layer] = total
         swf[layer] = swap_pairs(f)
 
+    for side in (0, 1):
+        y_copy(3, side).wait_recv()
+
+        @pl.loop(LX // 2 * side, LX // 2 * (side + 1))
+        def _(layer):
+            total = acc[layer]
+            for k in range(1, 7):
+                total = total + coeffs[k] * f3[HX + layer, pl.ds(HY + 2 * k * (1 - 2 * side), ROWS), :]
+            acc[layer] = total
+
     for piece in (0, 1):
         band_copy(0, piece).wait_recv()
         band_copy(2, piece).start()
-    y_copy(3, 0).wait_recv()
-
-    @pl.loop(0, LX)
-    def _(layer):
-        total = acc[layer]
-        for k in range(1, 7):
-            total = total + coeffs[k] * f3[HX + layer, pl.ds(HY + 2 * k, ROWS), :]
-        acc[layer] = total
 
     for piece, (first, count) in enumerate(PIECES):
         x_copy(3, piece, 0).wait_recv()
@@ -234,14 +239,13 @@
         products(1, near, piece)
     for piece in (0, 1):
         products(2, far, piece)
-    for piece in (0, 1):
+    for piece in range(2, NP):
+        band_copy(0, piece).wait_recv()
+        band_copy(2, piece).start()
+        products(2, far, piece)
+    for piece in range(NP):
         band_copy(2, piece).wait_recv()
         products(3, last, piece)
-    band_copy(0, 2).wait_recv()
-    band_copy(2, 2).start()
-    products(2, far, 2)
-    band_copy(2, 2).wait_recv()
-    products(3, last, 2)
 
     store = pltpu.make_async_copy(gathered, bands_ref, ls.at[2])
     store.start()
@@ -281,7 +285,7 @@
         for piece in range(NP):
             for side in (0, 1) if step < 3 else (0,):
                 x_copy(step, piece, side).wait_send()
-        for side in (0, 1) if step < 3 else (0,):
+        for side in (0, 1):
             y_copy(step, side).wait_send()
     for kind in range(3):
         for piece in range(NP):
@@ -289,12 +293,25 @@
     store.wait()
 
 
-def rotate_kernel(bands_ref, sums_ref, rotated_ref, density_ref, splat, mix, squares):
+def rotate_kernel(
+    bands_ref, sums_ref, rotated_ref, density_ref, bands, sums, rotated, density_out, splat, mix, squares,
+    in_sem, out_sem, sums_sem,
+):
     band = lax.axis_index("band")
+    parts_of = [pl.ds(PART * part, PART) for part in range(LX // PART)]
+    loads = [
+        pltpu.make_async_copy(bands_ref.at[:, layers], bands.at[:, layers], in_sem.at[part])
+        for part, layers in enumerate(parts_of)
+    ]
+    load_sums = pltpu.make_async_copy(sums_ref, sums, sums_sem.at[0])
+    load_sums.start()
+    for load in loads:
+        load.start()
+    load_sums.wait()
     highest = lax.Precision.HIGHEST
     row = lax.broadcasted_iota(jnp.int32, (128, 128), 0)
     lane = lax.broadcasted_iota(jnp.int32, (128, 128), 1)
-    diagonal = jnp.where(row == lane, jnp.broadcast_to(sums_ref[0:1, :], (128, 128)), 0.0)
+    diagonal = jnp.where(row == lane, jnp.broadcast_to(sums[0:1, :], (128, 128)), 0.0)
     splat[...] = jnp.dot(
         diagonal, jnp.ones((128, 128), jnp.float32), precision=highest, preferred_element_type=jnp.float32
     ) * (1.0 / 3538944.0)
@@ -348,26 +365,37 @@
             mix[8 * k + 2 * q] = jnp.where(even, columns[2 * q, 0], columns[2 * q + 1, 1])
             mix[8 * k + 2 * q + 1] = jnp.where(even, columns[2 * q + 1, 0], columns[2 * q, 1])
 
-    @pl.loop(0, LX)
-    def _(layer):
-        for tile in range(ROWS // 8):
-            rows = pl.ds(8 * tile, 8)
-            parts = []
-            for q in range(NB // 2):
-                g = bands_ref[q, layer, rows, :]
-                parts += [g, swap_pairs(g)]
-            density = own = None
-            for k in range(NB // 2):
-                v = mix[8 * k] * parts[0]
-                for n in range(1, 8):
-                    v = v + mix[8 * k + n] * parts[n]
-                density = v * v if density is None else density + v * v
-                own = v if own is None else jnp.where(band == k, v, own)
-            rotated_ref[layer, rows, :] = own
-            squares[rows, :] = density
-        density_ref[layer] = (
-            squares[pl.ds(0, LY, stride=2), :] + squares[pl.ds(1, LY, stride=2), :]
-        ) * (1.0 / NB)
+    stores = []
+    for part, layers in enumerate(parts_of):
+        loads[part].wait()
+
+        @pl.loop(PART * part, PART * (part + 1))
+        def _(layer):
+            for tile in range(ROWS // 8):
+                rows = pl.ds(8 * tile, 8)
+                parts = []
+                for q in range(NB // 2):
+                    g = bands[q, layer, rows, :]
+                    parts += [g, swap_pairs(g)]
+                density = own = None
+                for k in range(NB // 2):
+                    v = mix[8 * k] * parts[0]
+                    for n in range(1, 8):
+                        v = v + mix[8 * k + n] * parts[n]
+                    density = v * v if density is None else density + v * v
+                    own = v if own is None else jnp.where(band == k, v, own)
+                rotated[layer, rows, :] = own
+                squares[rows, :] = density
+            density_out[layer] = (
+                squares[pl.ds(0, LY, stride=2), :] + squares[pl.ds(1, LY, stride=2), :]
+            ) * (1.0 / NB)
+
+        for i, (src, dst) in enumerate(((rotated, rotated_ref), (density_out, density_ref))):
+            store = pltpu.make_async_copy(src.at[layers], dst.at[layers], out_sem.at[i, part])
+            store.start()
+            stores.append(store)
+    for store in stores:
+        store.wait()
 
 
 def on_device(orbitals, potential):
@@ -392,7 +420,7 @@
             dma((3, NP)), dma((3, NP)), dma((2, 15)), dma((2, 15)), dma((3,)),
         ],
         compiler_params=pltpu.CompilerParams(
-            collective_id=0, has_side_effects=True, vmem_limit_bytes=20 * 1024 * 1024
+            collective_id=0, has_side_effects=True, vmem_limit_bytes=VMEM_BYTES
         ),
         name="filter_and_sums",
     )(orb, potential)
@@ -402,10 +430,14 @@
             jax.ShapeDtypeStruct((LX, ROWS, 128), f32),
             jax.ShapeDtypeStruct((LX, LY, 128), f32),
         ),
-        in_specs=[pl.BlockSpec(memory_space=pltpu.VMEM)] * 2,
-        out_specs=(pl.BlockSpec(memory_space=pltpu.VMEM),) * 2,
-        scratch_shapes=[vmem((128, 128)), vmem((32, 8, 128)), vmem((ROWS, 128))],
-        compiler_params=pltpu.CompilerParams(vmem_limit_bytes=20 * 1024 * 1024),
+        in_specs=[pl.BlockSpec(memory_space=pl.ANY)] * 2,
+        out_specs=(pl.BlockSpec(memory_space=pl.ANY),) * 2,
+        scratch_shapes=[
+            vmem((4, LX, ROWS, 128)), vmem((8, 128)), block, vmem((LX, LY, 128)),
+            vmem((128, 128)), vmem((32, 8, 128)), vmem((ROWS, 128)),
+            dma((LX // PART,)), dma((2, LX // PART)), dma((1,)),
+        ],
+        compiler_params=pltpu.CompilerParams(vmem_limit_bytes=VMEM_BYTES),
         name="rotate_and_density",
     )(bands, sums)
     return rotated.reshape(LX, LY, 2, 128).transpose(2, 0, 1, 3), density

time: 55.3 us -> 51.2 us (0.926)
  Pallas kernels: 52.6 us -> 50.5 us
  local copies, waits for them, and re-layouts: 1.95 us -> 0 us
    pallas_call x1, Pallas kernels: 49.8 us -> 46.7 us  [on_device(): pl.pallas_call(filter_kernel, out_shape=(jax.ShapeDtypeStruct((4, LX, ROW...]
    unnamed x4 -> x0, local copies, waits for them, and re-layouts: 1.95 us -> none
    pallas_call x1, Pallas kernels: 2.73 us -> 3.75 us  [on_device(): pl.pallas_call(rotate_kernel, out_shape=(jax.ShapeDtypeStruct((LX, ROWS,...]
where the time goes in v1:
time: 51.2 us; the launch traced here: 51.1 us
  Pallas kernels  50.5 us (99%)
  between operations  0.64 us (1%)
    pallas_call x1, Pallas kernels, on_device(): pl.pallas_call(filter_kernel, out_shape=(jax.ShapeDtypeStruct((4, LX, ROW...  46.7 us
    pallas_call x1, Pallas kernels, on_device(): pl.pallas_call(rotate_kernel, out_shape=(jax.ShapeDtypeStruct((LX, ROWS,...  3.75 us

profile of v1, /device:TPU:1, one launch (start us, length us, event | category | flops | bytes accessed | tf_op | source)
XLA Modules:
  0.0 51.1 jit_solution(5242239091466714951)
XLA Ops:
  0.6 46.7 %filter_and_sums.1 = (f32[4,12,72,128]{3,2,1,0:T(8,128)}, f32[8,128]{1,0:T(8,128)}) custom-call(f32[12,72,128]{2,1,0:T(8,128)} %bitcast.6, f32[12,36,128]{2,1,0:T(8,128)} %pot_ref.1), custom_call_target="tpu_custom_call" | custom-call | tf_op jit(solution)/shard_map/filter_and_sums/pallas_call | solution.py:408
  47.4 3.7 %rotate_and_density.1 = (f32[12,72,128]{2,1,0:T(8,128)}, f32[12,36,128]{2,1,0:T(8,128)}) custom-call(f32[4,12,72,128]{3,2,1,0:T(8,128)} %get-tuple-element.6.bands_ref, f32[8,128]{1,0:T(8,128)} %get-tuple-element.7.sums_ref), custom_call_target="tpu_custom_call" | custom-call | tf_op jit(solution)/shard_map/rotate_and_density/pallas_call | solution.py:427

commit v2 on v1

--- a/solution.py
+++ b/solution.py
@@ -20,7 +20,7 @@
 HALFWIDTH = 4.75
 UPPER = 11.0
 NB = 8
-VMEM_BYTES = 60 * 1024 * 1024
+VMEM_BYTES = 56_400_000
 MESH = pl.DeviceIdType.MESH
 
 LX = 12
@@ -42,7 +42,7 @@
 
 def filter_kernel(
     orb_ref, pot_ref, bands_ref, sums_ref,
-    f0, f1, f2, f3, weight, pot, acc, app, swf, swa, gathered, accs, rows_a, rows_b, msg,
+    f0, f1, f2, f3, weight, pot, acc, zmat, app, swf, swa, near_app, near_swf, near_swa, gathered, accs, rows_a, rows_b, msg,
     xs, xr, ys, yr, ps, pr, gs, gr, ss, sr, ls,
 ):
     gx, gy, band = lax.axis_index("gx"), lax.axis_index("gy"), lax.axis_index("band")
@@ -100,15 +100,14 @@
 
     def band_copy(kind, piece):
         first, count = PIECES[piece]
-        mine = f3.at[pl.ds(HX, LX), pl.ds(HY + first, count)]
         rows = pl.ds(first, count)
-        if kind == 2:
-            src, slot = gathered.at[far, :, rows], far
+        if kind == 3:
+            src, dst = app.at[:, rows], near_app.at[:, rows]
+        elif kind == 2:
+            src = dst = gathered.at[far, :, rows]
         else:
-            src, slot = mine, band
-        return remote(
-            src, gathered.at[slot, :, rows], gs.at[kind, piece], gr.at[kind, piece], partner if kind == 0 else sibling
-        )
+            src, dst = f3.at[pl.ds(HX, LX), pl.ds(HY + first, count)], gathered.at[band, :, rows]
+        return remote(src, dst, gs.at[kind, piece], gr.at[kind, piece], partner if kind == 0 else sibling)
 
     def send_piece(step, piece):
         sides = (0,) if step == 3 else (0, 1)
@@ -122,6 +121,25 @@
             band_copy(0, piece).start()
             band_copy(1, piece).start()
 
+    offset = (lax.broadcasted_iota(jnp.int32, (128, 128), 0) - lax.broadcasted_iota(jnp.int32, (128, 128), 1)) & 127
+    for kind in (0, 1):
+        matrix = jnp.zeros((128, 128), jnp.float32)
+        for k in range(1, 7):
+            hit = (offset == k) if kind else (offset == k) | (offset == 128 - k)
+            matrix = jnp.where(hit, -(0.5 + 0.5 * kind) * COEFFS[k] / HALFWIDTH, matrix)
+        zmat[kind] = matrix
+
+    def local_terms(step, first, count):
+        rows = pl.ds(HY + first, count)
+        f = fields[step][pl.ds(HX, LX), rows, :]
+        along = jnp.dot(
+            f.reshape(-1, 128), zmat[step // 3], precision=lax.Precision.HIGHEST, preferred_element_type=jnp.float32
+        )
+        total = weight[:, pl.ds(first, count), :] * f + along.reshape(f.shape)
+        if step in (1, 2):
+            total = 2.0 * total - fields[step - 1][pl.ds(HX, LX), rows, :]
+        acc[step % 2, :, pl.ds(first, count), :] = total
+
     load_pot.wait()
     load_orb.wait()
 
@@ -131,6 +149,7 @@
         weight[layer, pl.ds(0, LY, stride=2), :] = values
         weight[layer, pl.ds(1, LY, stride=2), :] = values
 
+    local_terms(0, 0, ROWS)
     pl.semaphore_wait(barrier, 6)
     for piece in range(NP):
         send_piece(0, piece)
@@ -140,27 +159,17 @@
         scale = 1.0 if step == 0 else 2.0
         coeffs = [-0.5 * scale * c / HALFWIDTH for c in COEFFS]
 
+        y_copy(step, 0).wait_recv()
+        y_copy(step, 1).wait_recv()
+
         @pl.loop(0, LX)
         def _(layer):
-            f = field[HX + layer, pl.ds(HY, ROWS), :]
-            total = scale * weight[layer] * f
-            if step:
-                total = total - fields[step - 1][HX + layer, pl.ds(HY, ROWS), :]
-            for k in range(1, 7):
-                total = total + coeffs[k] * (pltpu.roll(f, k, 1) + pltpu.roll(f, 128 - k, 1))
-            acc[layer] = total
-
-        y_copy(step, 0).wait_recv()
-        y_copy(step, 1).wait_recv()
-
-        @pl.loop(0, LX)
-        def _(layer):
-            total = acc[layer]
+            total = acc[step % 2, layer]
             for k in range(1, 7):
                 below = field[HX + layer, pl.ds(HY - 2 * k, ROWS), :]
                 above = field[HX + layer, pl.ds(HY + 2 * k, ROWS), :]
                 total = total + coeffs[k] * (below + above)
-            acc[layer] = total
+            acc[step % 2, layer] = total
 
         for piece, (first, count) in enumerate(PIECES):
             x_copy(step, piece, 0).wait_recv()
@@ -169,48 +178,43 @@
 
             @pl.loop(0, LX)
             def _(layer):
-                total = acc[layer, pl.ds(first, count), :]
+                total = acc[step % 2, layer, pl.ds(first, count), :]
                 for k in range(1, 7):
                     total = total + coeffs[k] * (field[HX + layer - k, rows, :] + field[HX + layer + k, rows, :])
                 following[HX + layer, rows, :] = total
 
             send_piece(step + 1, piece)
+            local_terms(step + 1, first, count)
 
     coeffs = [-c / HALFWIDTH for c in COEFFS]
 
     @pl.loop(0, LX)
     def _(layer):
-        f = f3[HX + layer, pl.ds(HY, ROWS), :]
-        total = weight[layer] * f
-        for k in range(1, 7):
-            total = total + coeffs[k] * pltpu.roll(f, 128 - k, 1)
-        acc[layer] = total
-        swf[layer] = swap_pairs(f)
+        swf[layer] = swap_pairs(f3[HX + layer, pl.ds(HY, ROWS), :])
 
     for side in (0, 1):
         y_copy(3, side).wait_recv()
 
         @pl.loop(LX // 2 * side, LX // 2 * (side + 1))
         def _(layer):
-            total = acc[layer]
+            total = acc[1, layer]
             for k in range(1, 7):
                 total = total + coeffs[k] * f3[HX + layer, pl.ds(HY + 2 * k * (1 - 2 * side), ROWS), :]
-            acc[layer] = total
-
-    for piece in (0, 1):
-        band_copy(0, piece).wait_recv()
-        band_copy(2, piece).start()
+            acc[1, layer] = total
+
 
     for piece, (first, count) in enumerate(PIECES):
         x_copy(3, piece, 0).wait_recv()
 
         @pl.loop(0, LX)
         def _(layer):
-            total = acc[layer, pl.ds(first, count), :]
+            total = acc[1, layer, pl.ds(first, count), :]
             for k in range(1, 7):
                 total = total + coeffs[k] * f3[HX + layer + k, pl.ds(HY + first, count), :]
             app[layer, pl.ds(first, count), :] = total
             swa[layer, pl.ds(first, count), :] = swap_pairs(total)
+
+        band_copy(3, piece).start()
 
     accs[...] = jnp.zeros_like(accs)
 
@@ -225,7 +229,10 @@
             else:
                 g = gathered[slot, layer, rows, :]
             g = g.reshape(-1, 8, 128)
-            mine = (f3[HX + layer, pl.ds(HY + first, count), :], swf[layer, rows, :], app[layer, rows, :], swa[layer, rows, :])
+            if relative == 3:
+                mine = (gathered[near, layer, rows, :], near_swf[layer, rows, :], near_app[layer, rows, :], near_swa[layer, rows, :])
+            else:
+                mine = (f3[HX + layer, pl.ds(HY + first, count), :], swf[layer, rows, :], app[layer, rows, :], swa[layer, rows, :])
             return tuple(c + jnp.sum(m.reshape(-1, 8, 128) * g, axis=0) for c, m in zip(carry, mine))
 
         start = tuple(accs[pl.ds(8 * (4 * relative + i), 8), :] for i in range(4))
@@ -237,18 +244,21 @@
     for piece in range(NP):
         band_copy(1, piece).wait_recv()
         products(1, near, piece)
-    for piece in (0, 1):
+    for piece in range(NP):
+        band_copy(3, piece).wait_recv()
+
+    @pl.loop(0, LX)
+    def _(layer):
+        near_swf[layer] = swap_pairs(gathered[near, layer])
+        near_swa[layer] = swap_pairs(near_app[layer])
+
+    for piece in range(NP):
+        band_copy(0, piece).wait_recv()
         products(2, far, piece)
-    for piece in range(2, NP):
-        band_copy(0, piece).wait_recv()
-        band_copy(2, piece).start()
-        products(2, far, piece)
-    for piece in range(NP):
-        band_copy(2, piece).wait_recv()
-        products(3, last, piece)
-
-    store = pltpu.make_async_copy(gathered, bands_ref, ls.at[2])
-    store.start()
+        products(3, far, piece)
+
+    def store(slot, sem):
+        return pltpu.make_async_copy(gathered.at[slot], bands_ref.at[slot], ls.at[sem])
 
     highest = lax.Precision.HIGHEST
     by_row = lax.dot_general(
@@ -257,10 +267,18 @@
     )
     source = lax.broadcasted_iota(jnp.int32, (128, 128), 0)
     target = lax.broadcasted_iota(jnp.int32, (128, 128), 1)
-    place = (target == 32 * band + 2 * (source >> 3) + (source & 1)).astype(jnp.float32)
+    owner = jnp.where(source < 96, band, near)
+    place = (target == 32 * owner + 2 * (source >> 3) + (source & 1)).astype(jnp.float32)
     msg[pl.ds(0, 8), :] = jnp.dot(by_row, place, precision=highest, preferred_element_type=jnp.float32)
 
-    def sum_stage(stage, devices, me, rows):
+    def hand_on():
+        for piece in range(NP):
+            band_copy(2, piece).start()
+        store(band, 2).start()
+        store(near, 3).start()
+        store(far, 4).start()
+
+    def sum_stage(stage, devices, me, rows, meanwhile):
         rows[pl.ds(me, 1), :] = msg[pl.ds(8 * stage, 1), :]
         copies = [
             remote(msg.at[pl.ds(8 * stage, 1)], rows.at[pl.ds(me, 1)], ss.at[stage, i], sr.at[stage, i], device)
@@ -268,14 +286,21 @@
         ]
         for copy in copies:
             copy.start()
+        meanwhile()
         for copy in copies:
             copy.wait_recv()
         return copies
 
-    copies = sum_stage(0, group_a, 2 * gx + core, rows_a)
+    copies = sum_stage(0, group_a, 2 * gx + core, rows_a, hand_on)
     total = jnp.sum(rows_a[...], axis=0, keepdims=True)
     msg[pl.ds(8, 8), :] = jnp.broadcast_to(total, (8, 128))
-    copies = copies + sum_stage(1, group_b, 4 * (2 * y_hi + y_lo) + x, rows_b)
+
+    def take_last():
+        for piece in range(NP):
+            band_copy(2, piece).wait_recv()
+        store(last, 5).start()
+
+    copies = copies + sum_stage(1, group_b, 4 * (2 * y_hi + y_lo) + x, rows_b, take_last)
     total = jnp.sum(rows_b[...], axis=0, keepdims=True)
     sums_ref[...] = jnp.broadcast_to(total, (8, 128))
 
@@ -287,15 +312,15 @@
                 x_copy(step, piece, side).wait_send()
         for side in (0, 1):
             y_copy(step, side).wait_send()
-    for kind in range(3):
+    for kind in range(4):
         for piece in range(NP):
             band_copy(kind, piece).wait_send()
-    store.wait()
+    for slot, sem in ((band, 2), (near, 3), (far, 4), (last, 5)):
+        store(slot, sem).wait()
 
 
 def rotate_kernel(
-    bands_ref, sums_ref, rotated_ref, density_ref, bands, sums, rotated, density_out, splat, mix, squares,
-    in_sem, out_sem, sums_sem,
+    bands_ref, sums_ref, rotated_ref, density_ref, bands, rotated, density_out, splat, mix, squares, in_sem, out_sem
 ):
     band = lax.axis_index("band")
     parts_of = [pl.ds(PART * part, PART) for part in range(LX // PART)]
@@ -303,15 +328,12 @@
         pltpu.make_async_copy(bands_ref.at[:, layers], bands.at[:, layers], in_sem.at[part])
         for part, layers in enumerate(parts_of)
     ]
-    load_sums = pltpu.make_async_copy(sums_ref, sums, sums_sem.at[0])
-    load_sums.start()
     for load in loads:
         load.start()
-    load_sums.wait()
     highest = lax.Precision.HIGHEST
     row = lax.broadcasted_iota(jnp.int32, (128, 128), 0)
     lane = lax.broadcasted_iota(jnp.int32, (128, 128), 1)
-    diagonal = jnp.where(row == lane, jnp.broadcast_to(sums[0:1, :], (128, 128)), 0.0)
+    diagonal = jnp.where(row == lane, jnp.broadcast_to(sums_ref[0:1, :], (128, 128)), 0.0)
     splat[...] = jnp.dot(
         diagonal, jnp.ones((128, 128), jnp.float32), precision=highest, preferred_element_type=jnp.float32
     ) * (1.0 / 3538944.0)
@@ -414,10 +436,10 @@
         in_specs=[pl.BlockSpec(memory_space=pl.ANY)] * 2,
         out_specs=(pl.BlockSpec(memory_space=pl.ANY), pl.BlockSpec(memory_space=pltpu.VMEM)),
         scratch_shapes=[
-            field, field, field, field, block, vmem((LX, LY, 128)), block, block, block, block,
+            field, field, field, field, block, vmem((LX, LY, 128)), vmem((2, LX, ROWS, 128)), vmem((2, 128, 128)), block, block, block, block, block, block,
             vmem((4, LX, ROWS, 128)), vmem((128, 128)), vmem((16, 128)), vmem((16, 128)), vmem((16, 128)),
             dma((4, NP, 2)), dma((4, NP, 2)), dma((4, 2)), dma((4, 2)), dma((1,)), dma((1,)),
-            dma((3, NP)), dma((3, NP)), dma((2, 15)), dma((2, 15)), dma((3,)),
+            dma((4, NP)), dma((4, NP)), dma((2, 15)), dma((2, 15)), dma((6,)),
         ],
         compiler_params=pltpu.CompilerParams(
             collective_id=0, has_side_effects=True, vmem_limit_bytes=VMEM_BYTES
@@ -430,12 +452,12 @@
             jax.ShapeDtypeStruct((LX, ROWS, 128), f32),
             jax.ShapeDtypeStruct((LX, LY, 128), f32),
         ),
-        in_specs=[pl.BlockSpec(memory_space=pl.ANY)] * 2,
+        in_specs=[pl.BlockSpec(memory_space=pl.ANY), pl.BlockSpec(memory_space=pltpu.VMEM)],
         out_specs=(pl.BlockSpec(memory_space=pl.ANY),) * 2,
         scratch_shapes=[
-            vmem((4, LX, ROWS, 128)), vmem((8, 128)), block, vmem((LX, LY, 128)),
+            vmem((4, LX, ROWS, 128)), block, vmem((LX, LY, 128)),
             vmem((128, 128)), vmem((32, 8, 128)), vmem((ROWS, 128)),
-            dma((LX // PART,)), dma((2, LX // PART)), dma((1,)),
+            dma((LX // PART,)), dma((2, LX // PART)),
         ],
         compiler_params=pltpu.CompilerParams(vmem_limit_bytes=VMEM_BYTES),
         name="rotate_and_density",

time: 51.2 us -> 49.4 us (0.965)
  Pallas kernels: 50.5 us -> 48.6 us
    pallas_call x1, Pallas kernels: 46.7 us -> 45.5 us  [on_device(): pl.pallas_call(filter_kernel, out_shape=(jax.ShapeDtypeStruct((4, LX, ROW...]
    pallas_call x1, Pallas kernels: 3.75 us -> 3.18 us  [on_device(): pl.pallas_call(rotate_kernel, out_shape=(jax.ShapeDtypeStruct((LX, ROWS,...]
where the time goes in v2:
time: 49.4 us; the launch traced here: 49.3 us
  Pallas kernels  48.6 us (98%)
  between operations  0.64 us (1%)
    pallas_call x1, Pallas kernels, on_device(): pl.pallas_call(filter_kernel, out_shape=(jax.ShapeDtypeStruct((4, LX, ROW...  45.5 us
    pallas_call x1, Pallas kernels, on_device(): pl.pallas_call(rotate_kernel, out_shape=(jax.ShapeDtypeStruct((LX, ROWS,...  3.18 us

profile of v2, /device:TPU:1, one launch (start us, length us, event | category | flops | bytes accessed | tf_op | source)
XLA Modules:
  0.0 49.3 jit_solution(9019728757736168713)
XLA Ops:
  0.6 45.5 %filter_and_sums.1 = (f32[4,12,72,128]{3,2,1,0:T(8,128)}, f32[8,128]{1,0:T(8,128)S(1)}) custom-call(f32[12,72,128]{2,1,0:T(8,128)} %bitcast.6, f32[12,36,128]{2,1,0:T(8,128)} %pot_ref.1), custom_call_target="tpu_custom_call" | custom-call | tf_op jit(solution)/shard_map/filter_and_sums/pallas_call | solution.py:430
  46.1 3.2 %rotate_and_density.1 = (f32[12,72,128]{2,1,0:T(8,128)}, f32[12,36,128]{2,1,0:T(8,128)}) custom-call(f32[4,12,72,128]{3,2,1,0:T(8,128)} %get-tuple-element.6.bands_ref, f32[8,128]{1,0:T(8,128)S(1)} %get-tuple-element.7.sums_ref), custom_call_target="tpu_custom_call" | custom-call | tf_op jit(solution)/shard_map/rotate_and_density/pallas_call | solution.py:449

commit v3 on v2

--- a/solution.py
+++ b/solution.py
@@ -110,6 +110,8 @@
         return remote(src, dst, gs.at[kind, piece], gr.at[kind, piece], partner if kind == 0 else sibling)
 
     def send_piece(step, piece):
+        if step == 3:
+            band_copy(0, piece).start()
         sides = (0,) if step == 3 else (0, 1)
         for side in sides:
             x_copy(step, piece, side).start()
@@ -117,9 +119,6 @@
             y_copy(step, 0).start()
         if piece == 1:
             y_copy(step, 1).start()
-        if step == 3:
-            band_copy(0, piece).start()
-            band_copy(1, piece).start()
 
     offset = (lax.broadcasted_iota(jnp.int32, (128, 128), 0) - lax.broadcasted_iota(jnp.int32, (128, 128), 1)) & 127
     for kind in (0, 1):
@@ -159,6 +158,8 @@
         scale = 1.0 if step == 0 else 2.0
         coeffs = [-0.5 * scale * c / HALFWIDTH for c in COEFFS]
 
+        if step:
+            local_terms(step, 0, ROWS)
         y_copy(step, 0).wait_recv()
         y_copy(step, 1).wait_recv()
 
@@ -184,8 +185,10 @@
                 following[HX + layer, rows, :] = total
 
             send_piece(step + 1, piece)
-            local_terms(step + 1, first, count)
-
+
+    local_terms(3, 0, ROWS)
+    for piece in range(NP):
+        band_copy(1, piece).start()
     coeffs = [-c / HALFWIDTH for c in COEFFS]
 
     @pl.loop(0, LX)

time: 49.4 us -> 49.1 us (level)
  no operation moved by 1% of the time
where the time goes in v3:
time: 49.1 us; the launch traced here: 49 us
  Pallas kernels  48.4 us (99%)
  between operations  0.64 us (1%)
    pallas_call x1, Pallas kernels, on_device(): pl.pallas_call(filter_kernel, out_shape=(jax.ShapeDtypeStruct((4, LX, ROW...  45.2 us
    pallas_call x1, Pallas kernels, on_device(): pl.pallas_call(rotate_kernel, out_shape=(jax.ShapeDtypeStruct((LX, ROWS,...  3.18 us

profile of v3, /device:TPU:1, one launch (start us, length us, event | category | flops | bytes accessed | tf_op | source)
XLA Modules:
  0.0 49.0 jit_solution(16102882011887672196)
XLA Ops:
  0.6 45.2 %filter_and_sums.1 = (f32[4,12,72,128]{3,2,1,0:T(8,128)}, f32[8,128]{1,0:T(8,128)S(1)}) custom-call(f32[12,72,128]{2,1,0:T(8,128)} %bitcast.6, f32[12,36,128]{2,1,0:T(8,128)} %pot_ref.1), custom_call_target="tpu_custom_call" | custom-call | tf_op jit(solution)/shard_map/filter_and_sums/pallas_call | solution.py:433
  45.8 3.2 %rotate_and_density.1 = (f32[12,72,128]{2,1,0:T(8,128)}, f32[12,36,128]{2,1,0:T(8,128)}) custom-call(f32[4,12,72,128]{3,2,1,0:T(8,128)} %get-tuple-element.6.bands_ref, f32[8,128]{1,0:T(8,128)S(1)} %get-tuple-element.7.sums_ref), custom_call_target="tpu_custom_call" | custom-call | tf_op jit(solution)/shard_map/rotate_and_density/pallas_call | solution.py:452
